TPU v7x, 256 devices: a whole 4x4x8 slice. The times are simulated.
256 devices in a mesh: grp: 2 (over x_hi), wa: 128 (over z, x_lo, y, core).
Axes of the slice: x: 4 (x_hi: 2, x_lo: 2; x = x_hi * 2 + x_lo), y: 4, z: 8, core: 2. Of those that a mesh axis runs over, the one named last changes fastest.
Arguments:
- table: bfloat16 [1048576, 128], P(('grp', 'wa')), may hold values from -6 to 6
- owners: int32 [2, 16384, 8, 4], P('grp', 'wa'), may hold values from 0 to 127, all different within a row; in each aligned block of 1024 rows (0 to 1023, 1024 to 2047, ..., all dimensions but the last counted through in order) at most 64 rows name the same one
- local_rows: int32 [2, 16384, 8, 4], P('grp', 'wa'), may hold values from 0 to 4095
- lengths: int32 [2, 16384, 8], P('grp', 'wa'), may hold values from 2 to 4
- labels: float32 [16384], P('wa'), may hold values from 0 to 1
- w_first: bfloat16 [2048, 4096], P('grp'), may hold values from -0.125 to 0.125
- w_head: bfloat16 [4096], replicated, may hold values from -0.09375 to 0.09375
Outputs:
- logits: float32 [16384], P('wa')
- dense_grad: float32 [2048, 4096], P(('grp', 'wa'))
- head_grad: float32 [4096], P(('grp', 'wa'))
- row_grad: bfloat16 [1048576, 128], P(('grp', 'wa'))
Inputs may be any that keep to these rules, and one draw needn't show every extreme that they name: Within the 1024 bags of one device's samples, each owner is named at most 64 times, a bound that some block reaches; the 4 owners of one bag differ.
All inputs are finite; a program needn't handle non-finite values.
Results may differ from a plain program's by a relative error of at most 0.007.
Values may be sent and summed in bfloat16 or wider, within the bound.
No kernel may reach another device: no remote copies, remote signals or barrier semaphores. Data moves between devices by JAX's collectives and lax.ppermute only.
A program may use at most 128 MiB of HBM per device.

v0:
```python
import jax
import jax.numpy as jnp
from jax import lax
from jax.sharding import PartitionSpec as P


def silu_slope(values):
    gate = jax.nn.sigmoid(values)
    return gate * (1.0 + values * (1.0 - gate))


def shards(table, owners, local_rows, lengths, labels, w_first, w_head):
    owner_count = lax.axis_size("wa")
    samples = labels.shape[0]
    bags_here = owners.shape[2]
    depth = owners.shape[3]
    width = table.shape[1]
    hidden_width = w_head.shape[0]
    entries = samples * bags_here * depth
    capacity = max(2, 2 * entries // owner_count)
    owner_flat = owners.reshape(entries)
    local_flat = local_rows.reshape(entries)
    order_idx = jnp.argsort(owner_flat, stable=True)
    matches = (owner_flat[:, None] == jnp.arange(owner_count, dtype=jnp.int32)[None, :]).astype(
        jnp.int32
    )
    counts = jnp.sum(matches, axis=0)
    starts = jnp.cumsum(counts) - counts
    sorted_owner = owner_flat[order_idx]
    rank_sorted = jnp.arange(entries, dtype=jnp.int32) - starts[sorted_owner]
    position = jnp.zeros((entries,), jnp.int32).at[order_idx].set(rank_sorted)
    send_ids = (
        jnp.zeros((owner_count, capacity), jnp.int32).at[owner_flat, position].set(local_flat)
    )
    ids_in = lax.all_to_all(send_ids, "wa", split_axis=0, concat_axis=0, tiled=True)
    tiles = table[ids_in]
    returned = lax.all_to_all(tiles, "wa", split_axis=0, concat_axis=0, tiled=True)
    picked = (
        returned[owner_flat, position].reshape(samples, bags_here, depth, width).astype(jnp.float32)
    )
    live = jnp.arange(depth, dtype=jnp.int32)[None, None, :] < lengths[0][:, :, None]
    pooled = jnp.sum(jnp.where(live[..., None], picked, jnp.float32(0.0)), axis=2)
    pooled = pooled.astype(jnp.bfloat16).reshape(samples, bags_here * width)
    partial_value = jnp.dot(pooled, w_first, preferred_element_type=jnp.float32)
    group = lax.axis_index("grp")
    half = hidden_width // lax.axis_size("grp")
    pre = lax.psum(partial_value, "grp")
    hidden = jax.nn.silu(pre).astype(jnp.bfloat16)
    logits = jnp.dot(hidden, w_head, preferred_element_type=jnp.float32)
    dlogit = jax.nn.sigmoid(logits) - labels
    grad_hidden = (dlogit[:, None] * w_head.astype(jnp.float32)[None, :] * silu_slope(pre)).astype(
        jnp.bfloat16
    )
    head_term = jnp.dot(dlogit, hidden.astype(jnp.float32), precision=lax.Precision.HIGHEST)
    head_share = lax.dynamic_slice_in_dim(head_term, group * half, half)
    dense_term = lax.dot_general(
        pooled, grad_hidden, (((0,), (0,)), ((), ())), preferred_element_type=jnp.float32
    )
    dense_grad, head_grad = (
        lax.psum_scatter(dense_term, "wa", scatter_dimension=0, tiled=True),
        lax.psum_scatter(head_share, "wa", scatter_dimension=0, tiled=True),
    )
    pooled_grad = lax.dot_general(
        grad_hidden, w_first, (((1,), (1,)), ((), ())), preferred_element_type=jnp.float32
    )
    pooled_grad = pooled_grad.astype(jnp.bfloat16).reshape(samples, bags_here, 1, width)
    slot_grad = jnp.where(live[..., None], pooled_grad, jnp.bfloat16(0.0)).reshape(entries, width)
    send_grads = (
        jnp.zeros((owner_count, capacity, width), jnp.bfloat16)
        .at[owner_flat, position]
        .set(slot_grad)
    )
    arrived = lax.all_to_all(send_grads, "wa", split_axis=0, concat_axis=0, tiled=True)
    row_total = jnp.zeros((table.shape[0], width), jnp.float32)
    row_total = row_total.at[ids_in.reshape(-1)].add(arrived.reshape(-1, width).astype(jnp.float32))
    return (logits, dense_grad, head_grad, row_total.astype(jnp.bfloat16))


def solution(mesh):
    return jax.shard_map(
        shards,
        mesh=mesh,
        in_specs=(
            P(("grp", "wa"), None),
            P("grp", "wa", None, None),
            P("grp", "wa", None, None),
            P("grp", "wa", None),
            P("wa"),
            P("grp", None),
            P(),
        ),
        out_specs=(P("wa"), P(("grp", "wa"), None), P(("grp", "wa")), P(("grp", "wa"), None)),
        check_vma=False,
    )
```

profile of v0, /device:TPU:1, one launch (start us, length us, event | category | flops | bytes accessed | tf_op | source)
XLA Modules:
  0.0 953.8 jit_solution(7519618200322620608)
XLA Ops:
  7.2 1.1 copy.32
  8.8 1.9 convert_reduce_fusion
  10.7 5.8 sort.17
  16.5 23.0 %gather_fusion = s32[4096]{0:T(1024)S(1)} fusion(s32[4096]{0:T(1024)S(1)} %reshape.171, s32[4096]{0:T(1024)S(1)} %get-tuple-element.10), kind=kCustom, calls=%fused_computation | custom fusion | bytes 49152 | tf_op jit(solution)/shard_map/gather | solution.py:29
  40.0 24.7 %gather_fusion.1 = s32[4096]{0:T(1024)S(1)} fusion(s32[128]{0:T(128)S(1)} %sub.12, s32[4096]{0:T(1024)S(1)} %broadcast_clamp_fusion.1), kind=kCustom, calls=%fused_computation.1 | custom fusion | bytes 49152 | tf_op jit(solution)/shard_map/gather | solution.py:30
  64.8 15.5 %scatter_custom_fusion = s32[4096]{0:T(1024)S(1)} fusion(s32[4096]{0:T(1024)S(1)} %get-tuple-element.11, s32[4096]{0:T(1024)S(1)} %iota_subtract_fusion, s32[]{:T(128)} %constant.10.clone.1), kind=kCustom, calls=%fused_computation.52 | custom fusion | bytes 16388 | tf_op jit(solution)/shard_map/scatter | solution.py:31
  81.2 15.5 %scatter_custom_fusion.2 = s32[8192]{0:T(1024)S(1)} fusion(s32[4096]{0:T(1024)S(1)} %get-tuple-element.13, s32[4096]{0:T(1024)S(1)} %reshape.234, s32[]{:T(128)} %constant.10.clone.1), kind=kCustom, calls=%fused_computation.45 | custom fusion | bytes 32772
  96.9 25.3 %all_to_all.22 = s32[128,1,64]{2,1,0:T(1,128)S(1)} all-to-all(s32[128,1,64]{2,1,0:T(1,128)S(1)} %copy.36), channel_id=1, replica_groups=mesh['grp'=2,'wa'=128] {'wa'}, dimensions={0} | all-to-all | bytes 65536 | tf_op jit(solution)/shard_map/all_to_all | solution.py:35
  122.3 29.2 %gather_fusion.2 = bf16[8192,128]{1,0:T(8,128)(2,1)} fusion(bf16[4096,128]{1,0:T(8,128)(2,1)S(1)} %copy-done, s32[8192]{0:T(1024)S(1)} %broadcast_clamp_fusion), kind=kCustom, calls=%fused_computation.2 | custom fusion | bytes 4227072 | tf_op jit(solution)/shard_map/gather | solution.py:36
  151.5 6.0 all-to-all-start.1
  158.1 50.9 %all-to-all-done.1 = bf16[128,64,128]{2,1,0:T(8,128)(2,1)S(1)} async-done(((bf16[128,64,128]{2,1,0:T(8,128)(2,1)}), bf16[128,64,128]{2,1,0:T(8,128)(2,1)S(1)}, u32[]{:S(2)}, u32[]{:S(2)}) %all-to-all-start.1) | async-done | bytes 2097184 | tf_op jit(solution)/shard_map/all_to_all | solution.py:37
  209.0 40.5 %gather_fusion.3 = bf16[4096,128]{1,0:T(8,128)(2,1)} fusion(bf16[128,64,128]{2,1,0:T(8,128)(2,1)S(1)} %all-to-all-done.1, s32[4096]{0:T(1024)S(1)} %bitcast.52), kind=kCustom, calls=%fused_computation.3 | custom fusion | bytes 2129920 | tf_op jit(solution)/shard_map/gather | solution.py:39
  249.5 6.8 fusion.2
  256.4 6.0 fusion.12
  263.1 71.9 %all-reduce.3.cloned.1.call-done = f32[128,4096]{1,0:T(8,128)} async-done(((f32[128,4096]{1,0:T(8,128)}), f32[128,4096]{1,0:T(8,128)}) %all-reduce.3.cloned.1.call-update) | async-done | bytes 2097168 | tf_op jit(solution)/shard_map/psum | solution.py:47
  335.0 2.3 multiply_convert_fusion.1
  338.2 8.3 fusion.10
  346.9 6.9 fusion.3
  354.2 14.6 %scatter_custom_fusion.3 = bf16[8192,128]{1,0:T(8,128)(2,1)} fusion(s32[4096]{0:T(1024)S(1)} %get-tuple-element.12, bf16[]{:T(256)} %constant.19.clone.1, bf16[4096,128]{1,0:T(8,128)(2,1)S(1)} %bitcast.55, pred[4096]{0:T(1024)(128)(4,1)S(1)} %lt.92), kind=kCustom, calls=%fused_computation.20 | custom fusion | flops 524288 | bytes 3150848
  368.9 12.3 %all-to-all-start.2 = ((bf16[128,64,128]{2,1,0:T(8,128)(2,1)}), bf16[128,64,128]{2,1,0:T(8,128)(2,1)}, u32[]{:S(2)}, u32[]{:S(2)}) async-start(bf16[128,64,128]{2,1,0:T(8,128)(2,1)} %bitcast.54), calls=%async_computation.3 | async-start | bytes 4194304 | tf_op jit(solution)/shard_map/all_to_all | solution.py:73
  384.4 321.0 %all-reduce = f32[2048]{0:T(1024)S(1)} all-reduce(f32[2048]{0:T(1024)S(1)} %dynamic_slice.3), channel_id=3, replica_groups=mesh['grp'=2,'wa'=128] {'wa'}, use_global_device_ids=true, to_apply=%region_8.9.clone | all-reduce | flops 2048 | bytes 16384
  706.1 49.4 %scatter_custom_fusion.1 = f32[4096,128]{1,0:T(8,128)S(1)} fusion(s32[8192]{0:T(1024)S(1)} %bitcast.68, bf16[8192,128]{1,0:T(8,128)(2,1)} %bitcast.23, f32[]{:T(128)} %constant.14.clone.1), kind=kCustom, calls=%fused_computation.8 | custom fusion | flops 2097152 | bytes 4194308 | tf_op jit(solution)/shard_map/scatter-add | solution.py:75
  755.5 1.1 convert_element_type.49
  756.6 190.4 %reduce-scatter.2.cloned.1.call-done = f32[8,4096]{1,0:T(8,128)} async-done(((f32[1024,4096]{1,0:T(8,128)}), f32[8,4096]{1,0:T(8,128)}) %reduce-scatter.2.cloned.1.call-update) | async-done | bytes 131088 | tf_op jit(solution)/shard_map/reduce_scatter | solution.py:60
  (63 shorter events, 8.2 us)
Async XLA Ops:
  7.2 115.1 %copy-start = (bf16[4096,128]{1,0:T(8,128)(2,1)S(1)}, bf16[4096,128]{1,0:T(8,128)(2,1)}, u32[]{:S(2)}) copy-start(bf16[4096,128]{1,0:T(8,128)(2,1)} %param.7) | copy-start | bytes 3145732
  40.0 40.3 %copy-start.3 = (s32[1,128,8,4]{1,3,2,0:T(4,128)S(1)}, s32[1,128,8,4]{1,3,2,0:T(4,128)}, u32[]{:S(2)}) copy-start(s32[1,128,8,4]{1,3,2,0:T(4,128)} %param.9) | copy-start | bytes 49156
  40.0 40.9 %copy-start.8 = (s32[2]{0:T(128)S(1)}, s32[2]{0:T(128)}, u32[]{:S(2)}) copy-start(s32[2]{0:T(128)} %constant.42) | copy-start | bytes 28
  40.0 41.0 %copy-start.6 = (s32[2]{0:T(128)S(1)}, s32[2]{0:T(128)}, u32[]{:S(2)}) copy-start(s32[2]{0:T(128)} %constant.45) | copy-start | bytes 28
  40.0 41.0 %copy-start.7 = (s32[2]{0:T(128)S(1)}, s32[2]{0:T(128)}, u32[]{:S(2)}) copy-start(s32[2]{0:T(128)} %constant.8) | copy-start | bytes 28
  151.5 6.2 copy-start.4
  151.5 57.5 %all-to-all-start.1 = ((bf16[128,64,128]{2,1,0:T(8,128)(2,1)}), bf16[128,64,128]{2,1,0:T(8,128)(2,1)S(1)}, u32[]{:S(2)}, u32[]{:S(2)}) async-start(bf16[128,64,128]{2,1,0:T(8,128)(2,1)} %bitcast.53), calls=%async_computation.1 | async-start | bytes 4194304 | tf_op jit(solution)/shard_map/all_to_all | solution.py:37
  157.5 177.5 %all-reduce.3.cloned.1.call-start = ((), (), s32[]{:S(2)}) async-start(), calls=%async_computation.4 | async-start | bytes 4194304 | tf_op jit(solution)/shard_map/psum | solution.py:47
  262.4 0.7 copy-start.2
  262.4 74.9 %copy-start.5 = (f32[128]{0:T(128)S(1)}, f32[128]{0:T(128)}, u32[]{:S(2)}) copy-start(f32[128]{0:T(128)} %param.11) | copy-start | bytes 1540
  262.4 684.6 %reduce-scatter.2.cloned.1.call-start = ((), (), s32[]{:S(2)}) async-start(), calls=%async_computation.5 | async-start | bytes 16908288 | tf_op jit(solution)/shard_map/reduce_scatter | solution.py:60
  335.0 3.2 copy-start.1
  368.9 12.3 %copy-start.9 = (u32[256]{0:T(256)S(1)}, u32[256]{0:T(256)}, u32[]{:S(2)}) copy-start(u32[256]{0:T(256)} %constant.69) | copy-start | bytes 3076
  368.9 337.2 %all-to-all-start.2 = ((bf16[128,64,128]{2,1,0:T(8,128)(2,1)}), bf16[128,64,128]{2,1,0:T(8,128)(2,1)}, u32[]{:S(2)}, u32[]{:S(2)}) async-start(bf16[128,64,128]{2,1,0:T(8,128)(2,1)} %bitcast.54), calls=%async_computation.3 | async-start | bytes 4194304 | tf_op jit(solution)/shard_map/all_to_all | solution.py:73
Sparse Core Ops, SparseCore 0:
  262.5 72.4 all-reduce.2
  346.6 600.2 reduce-scatter.1
where the time goes:
time: 957 us; the launch traced here: 954 us
  blocking collectives  346 us (36%)
  waiting for transfers between devices  313 us (33%)
  local copies, waits for them, and re-layouts  154 us (16%)
  other arithmetic  83.6 us (9%)
  matrix products  22.7 us (2%)
  starting transfers between devices  18.6 us (2%)
  between operations  15 us (2%)
    unnamed x1, blocking collectives  321 us
    reduce_scatter x1, waiting for transfers between devices, shards(): lax.psum_scatter(dense_term, 'wa', scatter_dimension=0, tiled=True)  190 us
    psum x1, waiting for transfers between devices, shards(): pre = lax.psum(partial_value, 'grp')  71.9 us
    all_to_all x1, waiting for transfers between devices, shards(): lax.all_to_all(tiles, 'wa', split_axis=0, concat_axis=0, tiled=True)  50.9 us
    scatter-add x1, other arithmetic, shards(): row_total.at[ids_in.reshape(-1)]  49.4 us
    gather x1, local copies, waits for them, and re-layouts, shards(): returned[owner_flat, position].reshape(samples, bags_here, depth, width)  40.5 us
    gather x1, local copies, waits for them, and re-layouts, shards(): tiles = table[ids_in]  29.2 us
    all_to_all x1, blocking collectives, shards(): lax.all_to_all(send_ids, 'wa', split_axis=0, concat_axis=0, tiled=True)  25.3 us
  transfers between devices with their start and end apart: 4, of which 3 were waited for; matrix products, arithmetic and copies ran while one was open for 8% of the time, Pallas kernels for 0%

commit v1 on v0

v1 whole, which is shorter than its diff:
```python
import functools

import jax
import jax.numpy as jnp
from jax import lax
from jax.experimental import pallas as pl
from jax.experimental.pallas import tpu as pltpu
from jax.sharding import PartitionSpec as P

BF16 = jnp.bfloat16
F32 = jnp.float32
I32 = jnp.int32
E = 128
CAP = 64
ROWS_BITS = 12
LIMIT = pltpu.CompilerParams(vmem_limit_bytes=56 * 1024 * 1024)
NT = (((1,), (1,)), ((), ()))


def one_hot(left, right):
    return jnp.where(left == right, 1.0, 0.0).astype(BF16)


def route_kernel(code_ref, ids_ref, bag_ref, bag_t_ref):
    lines = code_ref.shape[0]
    owners = ids_ref.shape[0]
    pairs = owners // 2
    sub = lax.broadcasted_iota(I32, (owners, E), 0)
    half_sub = lax.broadcasted_iota(I32, (CAP, E), 0)
    pair_sub = lax.broadcasted_iota(I32, (pairs, E), 0)
    lane = lax.broadcasted_iota(I32, (1, E), 1)
    before = one_hot(
        jnp.where(lax.broadcasted_iota(I32, (E, E), 0) < lax.broadcasted_iota(I32, (E, E), 1), 1, 0), 1
    )
    features = lines // 4
    carry = jnp.zeros((owners, 1), F32)
    ids_hi = jnp.zeros((owners, CAP), F32)
    ids_lo = jnp.zeros((owners, CAP), F32)
    bag = jnp.zeros((pairs, 2 * E), F32)
    bag_t = jnp.zeros((2 * E, pairs), F32)
    for k in range(lines):
        code = code_ref[k : k + 1, :]
        owner = code >> ROWS_BITS
        local = code & ((1 << ROWS_BITS) - 1)
        number = (k % features) * E + lane + 1
        named = jnp.where(sub == owner, 1.0, 0.0)
        named_b = named.astype(BF16)
        rank = jnp.dot(named_b, before, preferred_element_type=F32) + carry
        carry = carry + jnp.sum(named, axis=1, keepdims=True)
        position = jnp.sum(named * rank, axis=0, keepdims=True).astype(I32)
        place = jnp.where(half_sub == position, 1.0, 0.0)
        place_hi = (place * (local >> 6).astype(F32)).astype(BF16)
        place_lo = (place * (local & 63).astype(F32)).astype(BF16)
        ids_hi += lax.dot_general(named_b, place_hi, NT, preferred_element_type=F32)
        ids_lo += lax.dot_general(named_b, place_lo, NT, preferred_element_type=F32)
        spot = jnp.where(sub == (owner & 1) * CAP + position, 1.0, 0.0)
        spot2 = jnp.concatenate(
            [(spot * (number >> 5).astype(F32)).astype(BF16), (spot * (number & 31).astype(F32)).astype(BF16)], axis=0
        )
        in_pair = one_hot(pair_sub, owner >> 1)
        bag += lax.dot_general(in_pair, spot2, NT, preferred_element_type=F32)
        bag_t += lax.dot_general(spot2, in_pair, NT, preferred_element_type=F32)
    ids_ref[...] = (ids_hi * 64.0 + ids_lo).astype(I32)
    bag_ref[...] = (bag[:, :E] * 32.0 + bag[:, E:]).astype(I32) - 1
    bag_t_ref[...] = (bag_t[:E, :] * 32.0 + bag_t[E:, :]).astype(I32) - 1


def gather_kernel(ids_ref, table_ref, out_ref, spread):
    sources = ids_ref.shape[0]
    ids_t = jnp.transpose(ids_ref[...].astype(F32)).astype(I32)
    for s in range(sources):
        spread[s * CAP : (s + 1) * CAP, :] = jnp.broadcast_to(ids_t[:, s : s + 1], (CAP, E))
    rows = table_ref.shape[0]
    block = 1024
    depth = 1024
    lane = lax.broadcasted_iota(I32, (1, E), 1)

    def body(i, _):
        wanted = spread[pl.ds(pl.multiple_of(i * block, block), block), :]
        total = jnp.zeros((block, E), F32)
        for d in range(rows // depth):
            parts = [one_hot(wanted, lane + (d * depth + m * E)) for m in range(depth // E)]
            total += jnp.dot(
                jnp.concatenate(parts, axis=1),
                table_ref[d * depth : (d + 1) * depth, :],
                preferred_element_type=F32,
            )
        out_ref[pl.ds(pl.multiple_of(i * block, block), block), :] = total.astype(BF16)
        return 0

    lax.fori_loop(0, sources * CAP // block, body, 0)


def sum_rows(lists_ref, data_ref, base, count):
    chunk = 8
    sub = lax.broadcasted_iota(I32, (count, E), 0) + base

    def body(i, total):
        lists = lists_ref[pl.ds(pl.multiple_of(i * chunk, chunk), chunk), :]
        parts = [one_hot(sub, lists[m : m + 1, :]) for m in range(chunk)]
        return total + jnp.dot(
            jnp.concatenate(parts, axis=1),
            data_ref[pl.ds(pl.multiple_of(i * chunk * E, chunk * E), chunk * E), :],
            preferred_element_type=F32,
        )

    return lax.fori_loop(0, lists_ref.shape[0] // chunk, body, jnp.zeros((count, E), F32))


def pool_kernel(bag_ref, rows_ref, w_ref, pooled_ref, part_ref):
    bags = pooled_ref.shape[1] // E * pooled_ref.shape[0]
    samples = pooled_ref.shape[0]
    pooled = sum_rows(bag_ref, rows_ref, 0, bags).astype(BF16)
    for f in range(bags // samples):
        pooled_ref[:, f * E : (f + 1) * E] = pooled[f * samples : (f + 1) * samples, :]
    step = 512
    for j in range(w_ref.shape[1] // step):
        part_ref[:, j * step : (j + 1) * step] = jnp.dot(
            pooled_ref[...], w_ref[:, j * step : (j + 1) * step], preferred_element_type=F32
        ).astype(BF16)


def head_kernel(mine_ref, other_ref, labels_ref, w_head_ref, logits_ref, grad_ref, head_ref):
    pieces, samples, width = grad_ref.shape
    logits = jnp.zeros((samples, 1), F32)
    for q in range(pieces):
        cols = slice(q * width, (q + 1) * width)
        pre = mine_ref[:, cols].astype(F32) + other_ref[:, cols].astype(F32)
        hidden = (pre * jax.nn.sigmoid(pre)).astype(BF16).astype(F32)
        logits += jnp.sum(hidden * w_head_ref[:, cols].astype(F32), axis=1, keepdims=True)
    logits_ref[...] = logits
    dlogit = jax.nn.sigmoid(logits) - labels_ref[...]
    for q in range(pieces):
        cols = slice(q * width, (q + 1) * width)
        pre = mine_ref[:, cols].astype(F32) + other_ref[:, cols].astype(F32)
        gate = jax.nn.sigmoid(pre)
        hidden = (pre * gate).astype(BF16).astype(F32)
        head_ref[:, cols] = jnp.sum(hidden * dlogit, axis=0, keepdims=True)
        slope = gate * (1.0 + pre * (1.0 - gate))
        grad_ref[q] = (dlogit * w_head_ref[:, cols].astype(F32) * slope).astype(BF16)


def back_kernel(grad_ref, w_ref, bag_t_ref, out_ref, pooled_grad):
    pieces, samples, width = grad_ref.shape
    bags = pooled_grad.shape[0]
    half = w_ref.shape[0] // 2
    for h in range(2):
        total = jnp.zeros((samples, half), F32)
        for q in range(pieces):
            total += lax.dot_general(
                grad_ref[q],
                w_ref[h * half : (h + 1) * half, q * width : (q + 1) * width],
                NT,
                preferred_element_type=F32,
            )
        for f in range(half // E):
            b = h * (half // E) + f
            pooled_grad[b * samples : (b + 1) * samples, :] = total[:, f * E : (f + 1) * E].astype(BF16)
    lane = lax.broadcasted_iota(I32, (1, E), 1)
    together = 8
    for k in range(0, bag_t_ref.shape[1], together):
        wanted = jnp.concatenate(
            [jnp.broadcast_to(bag_t_ref[:, k + m : k + m + 1], (E, E)) for m in range(together)], axis=0
        )
        parts = [one_hot(wanted, lane + b * E) for b in range(bags // E)]
        out_ref[k * E : (k + together) * E, :] = jnp.dot(
            jnp.concatenate(parts, axis=1), pooled_grad[...], preferred_element_type=F32
        ).astype(BF16)


def dense_kernel(*refs):
    out_ref = refs[-1]
    count = (len(refs) - 1) // 2
    features = [r for r in refs[:count]]
    grads = [r for r in refs[count : 2 * count]]
    left = jnp.concatenate([r[...].reshape(-1, r.shape[-1]) for r in features], axis=0)
    right = jnp.concatenate([r[...].reshape(-1, r.shape[-1]) for r in grads], axis=0)
    out_ref[...] = lax.dot_general(
        left, right, (((0,), (0,)), ((), ())), preferred_element_type=F32
    ).astype(out_ref.dtype)


def scatter_kernel(ids_ref, data_ref, out_ref):
    rows = out_ref.shape[0]
    block = 1024

    def body(i, _):
        start = pl.multiple_of(i * block, block)
        out_ref[pl.ds(start, block), :] = sum_rows(ids_ref, data_ref, i * block, block).astype(BF16)
        return 0

    lax.fori_loop(0, rows // block, body, 0)


def call(kernel, outs, flops, moved, scratch=()):
    return pl.pallas_call(
        kernel,
        out_shape=outs,
        scratch_shapes=list(scratch),
        compiler_params=LIMIT,
        cost_estimate=pl.CostEstimate(flops=flops, bytes_accessed=moved, transcendentals=0),
    )


def shape(dims, kind):
    return jax.ShapeDtypeStruct(dims, kind)


def shards(table, owners, local_rows, lengths, labels, w_first, w_head):
    count = lax.axis_size("wa")
    samples = labels.shape[0]
    bags_here = owners.shape[2]
    depth = owners.shape[3]
    hidden_width = w_head.shape[0]
    feats = bags_here * E
    slots = count * CAP
    place = lax.axis_index("wa")
    group = lax.axis_index("grp")
    y = (place // 2) % 4
    core = place % 2
    x_low = (place // 8) % 2

    def spot(z, x, yy, c):
        return ((z * 2 + x) * 4 + yy % 4) * 2 + c

    def where_of(w):
        return w // 16, (w // 8) % 2, (w // 2) % 4, w % 2

    def moved(step):
        return [(w, spot(*step(*where_of(w)))) for w in range(count)]

    to_mate = moved(lambda z, x, yy, c: (z, x, yy, 1 - c))
    to_x = moved(lambda z, x, yy, c: (z, 1 - x, yy, c))
    to_y = [moved(lambda z, x, yy, c, d=d: (z, x, yy + d, c)) for d in (1, 3, 2)]
    z_groups = [[z * 16 + r for z in range(8)] for r in range(16)]
    yc_groups = [[g * 8 + r for r in range(8)] for g in range(16)]

    live = jnp.arange(depth, dtype=I32) < lengths[0][:, :, None]
    code = jnp.where(live, owners[0] * (1 << ROWS_BITS) + local_rows[0], -1)
    code = jnp.transpose(code, (2, 1, 0)).reshape(depth * bags_here, samples)
    ids, bag, bag_t = call(
        route_kernel,
        (shape((count, CAP), I32), shape((count // 2, 2 * CAP), I32), shape((2 * CAP, count // 2), I32)),
        2 * 4096 * 128 * 1024,
        100000,
    )(code)
    ids_in = lax.all_to_all(ids, "wa", split_axis=0, concat_axis=0, tiled=True)
    tiles = call(
        gather_kernel,
        shape((slots, E), BF16),
        2 * slots * 4096 * E,
        4 << 20,
        [pltpu.VMEM((slots, E), I32)],
    )(ids_in, table)
    returned = lax.all_to_all(
        tiles.reshape(count, CAP, E), "wa", split_axis=0, concat_axis=0, tiled=True
    ).reshape(slots, E)
    pooled, part = call(
        pool_kernel,
        (shape((samples, feats), BF16), shape((samples, hidden_width), BF16)),
        2 * slots * 1024 * E + 2 * samples * feats * hidden_width,
        12 << 20,
    )(bag, returned, w_first)
    other = lax.ppermute(part, "grp", [(0, 1), (1, 0)])

    mate_pooled = lax.ppermute(pooled, "wa", to_mate)
    both_pooled = jnp.concatenate([pooled, mate_pooled], axis=0)
    all_pooled = [both_pooled] + [lax.ppermute(both_pooled, "wa", p) for p in to_y]

    logits, grad, head = call(
        head_kernel,
        (
            shape((samples, 1), F32),
            shape((8, samples, hidden_width // 8), BF16),
            shape((1, hidden_width), F32),
        ),
        samples * hidden_width * 60,
        4 << 20,
    )(part, other, labels.reshape(samples, 1), w_head.reshape(1, hidden_width))

    width = hidden_width // 8
    grad4 = grad.reshape(4, 2, samples, width)
    keep = lax.dynamic_index_in_dim(grad4, core, 1, False)
    mate_grad = lax.ppermute(lax.dynamic_index_in_dim(grad4, 1 - core, 1, False), "wa", to_mate)
    pairs = jnp.concatenate([keep, mate_grad], axis=1)

    def piece(d):
        return lax.dynamic_index_in_dim(pairs, (y + d) % 4, 0, False)

    all_grad = [piece(0)] + [lax.ppermute(piece(d), "wa", p) for d, p in zip((1, 3, 2), to_y)]

    send = call(
        back_kernel,
        shape((slots, E), BF16),
        2 * slots * 1024 * E + 2 * samples * feats * hidden_width,
        12 << 20,
        [pltpu.VMEM((samples * bags_here, E), BF16)],
    )(grad, w_first, bag_t)
    arrived = lax.all_to_all(
        send.reshape(count, CAP, E), "wa", split_axis=0, concat_axis=0, tiled=True
    ).reshape(slots, E)

    dense = call(
        dense_kernel, shape((feats, width), BF16), 2 * feats * width * 8 * samples, 4 << 20
    )(*all_pooled, *all_grad)
    dense = dense.reshape(8, 2, feats // 16, width)
    mine = lax.dynamic_index_in_dim(dense, x_low, 1, False)
    theirs = lax.ppermute(lax.dynamic_index_in_dim(dense, 1 - x_low, 1, False), "wa", to_x)
    partial = (mine.astype(F32) + theirs.astype(F32)).astype(BF16)
    by_z = lax.all_to_all(partial, "wa", 0, 0, axis_index_groups=z_groups, tiled=True)
    block = jnp.sum(by_z.astype(F32), axis=0).reshape(8, 8, width)
    turned = lax.all_to_all(block, "wa", 0, 0, axis_index_groups=yc_groups, tiled=True)
    dense_grad = jnp.transpose(turned, (1, 0, 2)).reshape(8, hidden_width)

    head_share = lax.dynamic_slice_in_dim(head[0], group * (hidden_width // 2), hidden_width // 2)
    head_in = lax.all_to_all(
        head_share.reshape(count, hidden_width // 2 // count), "wa", split_axis=0, concat_axis=0, tiled=True
    )
    head_grad = jnp.sum(head_in, axis=0)

    row_grad = call(
        scatter_kernel, shape((table.shape[0], E), BF16), 2 * slots * 4096 * E, 4 << 20
    )(ids_in.reshape(count // 2, 2 * CAP), arrived)
    return (logits.reshape(samples), dense_grad, head_grad, row_grad)


def solution(mesh):
    return jax.shard_map(
        shards,
        mesh=mesh,
        in_specs=(
            P(("grp", "wa"), None),
            P("grp", "wa", None, None),
            P("grp", "wa", None, None),
            P("grp", "wa", None),
            P("wa"),
            P("grp", None),
            P(),
        ),
        out_specs=(P("wa"), P(("grp", "wa"), None), P(("grp", "wa")), P(("grp", "wa"), None)),
        check_vma=False,
    )
```

time: 957 us -> 364 us (0.38)
  blocking collectives: 346 us -> 83.8 us
  waiting for transfers between devices: 313 us -> 136 us
  local copies, waits for them, and re-layouts: 154 us -> 10 us
  Pallas kernels: 0 us -> 91 us
  other arithmetic: 83.6 us -> 6.43 us
  matrix products: 22.7 us -> 0 us
  starting transfers between devices: 18.6 us -> 35.2 us
  between operations: 15 us -> 0.79 us
    unnamed x1 -> x0, blocking collectives: 321 us -> none
    reduce_scatter x1 -> x0, waiting for transfers between devices: 190 us -> none  [shards(): lax.psum_scatter(dense_term, 'wa', scatter_dimension=0, tiled=True)]
    gather x4 -> x0, local copies, waits for them, and re-layouts: 118 us -> none  [the longest x1 40.5 us: shards(): returned[owner_flat, position].reshape(samples, bags_here, depth, width)]
    pallas_call x0 -> x7, Pallas kernels: none -> 91 us  [the longest x1 27.1 us: shards(): call(scatter_kernel, shape((table.shape[0], E), BF16), 2 * slots * 4096 *...]
    psum x1 -> x0, waiting for transfers between devices: 71.9 us -> none  [shards(): pre = lax.psum(partial_value, 'grp')]
    ppermute x0 -> x10, waiting for transfers between devices: none -> 63 us  [the longest x1 21.6 us: shards(): other = lax.ppermute(part, 'grp', [(0, 1), (1, 0)])]
    all_to_all x1 -> x2, blocking collectives: 25.3 us -> 83.8 us  [the longest x1 58 us: shards(): lax.all_to_all(tiles.reshape(count, CAP, E), 'wa', split_axis=0, concat_a...]
    scatter-add x1 -> x0, other arithmetic: 49.4 us -> none  [shards(): row_total.at[ids_in.reshape(-1)]]
  transfers between devices with their start and end apart: 4 -> 14, of which waited for: 3 -> 11; matrix products, arithmetic and copies ran while one was open for 8% -> 2% of each run, Pallas kernels for 0% -> 4%
where the time goes in v1:
time: 364 us; the launch traced here: 363 us
  waiting for transfers between devices  136 us (37%)
  Pallas kernels  91 us (25%)
  blocking collectives  83.8 us (23%)
  starting transfers between devices  35.2 us (10%)
  local copies, waits for them, and re-layouts  10 us (3%)
  other arithmetic  6.43 us (2%)
    all_to_all x1, blocking collectives, shards(): lax.all_to_all(tiles.reshape(count, CAP, E), 'wa', split_axis=0, concat_a...  58 us
    all_to_all x1, waiting for transfers between devices, shards(): lax.all_to_all(send.reshape(count, CAP, E), 'wa', split_axis=0, concat_ax...  48 us
    pallas_call x1, Pallas kernels, shards(): call(scatter_kernel, shape((table.shape[0], E), BF16), 2 * slots * 4096 *...  27.1 us
    all_to_all x1, blocking collectives, shards(): ids_in = lax.all_to_all(ids, 'wa', split_axis=0, concat_axis=0, tiled=True)  25.8 us
    pallas_call x1, Pallas kernels, shards(): call(gather_kernel, shape((slots, E), BF16), 2 * slots * 4096 * E, 4 << 2...  22.6 us
    ppermute x1, waiting for transfers between devices, shards(): other = lax.ppermute(part, 'grp', [(0, 1), (1, 0)])  21.6 us
    ppermute x3, waiting for transfers between devices, shards(): lax.ppermute(both_pooled, 'wa', p)  18.9 us
    all_to_all x1, waiting for transfers between devices, shards(): lax.all_to_all(partial, 'wa', 0, 0, axis_index_groups=z_groups, tiled=True)  15.1 us
  transfers between devices with their start and end apart: 14, of which 11 were waited for; matrix products, arithmetic and copies ran while one was open for 2% of the time, Pallas kernels for 4%

profile of v1, /device:TPU:1, one launch (start us, length us, event | category | flops | bytes accessed | tf_op | source)
XLA Modules:
  0.0 363.2 jit_solution(10478672909176344642)
XLA Ops:
  2.0 8.7 %shard_map.102 = (s32[128,64]{1,0:T(8,128)}, s32[64,128]{1,0:T(8,128)}, s32[128,64]{1,0:T(8,128)}) custom-call(s32[32,128]{1,0:T(8,128)} %bitcast.53), custom_call_target="tpu_custom_call" | custom-call | flops 1073741824 | bytes 100000 | tf_op jit(solution)/shard_map/pallas_call | solution.py:241
  10.7 25.8 %all_to_all.40 = s32[128,1,64]{2,1,0:T(1,128)} all-to-all(s32[128,1,64]{2,1,0:T(1,128)} %bitcast.52), channel_id=1, replica_groups=mesh['grp'=2,'wa'=128] {'wa'}, dimensions={0} | all-to-all | bytes 65536 | tf_op jit(solution)/shard_map/all_to_all | solution.py:247
  36.5 22.6 %shard_map.103 = bf16[8192,128]{1,0:T(8,128)(2,1)} custom-call(s32[128,64]{1,0:T(8,128)} %bitcast.51, bf16[4096,128]{1,0:T(8,128)(2,1)} %table_ref.1), custom_call_target="tpu_custom_call" | custom-call | flops 8589934592 | bytes 4194304 | tf_op jit(solution)/shard_map/pallas_call | solution.py:248
  59.1 58.0 %all_to_all.41 = bf16[128,64,128]{2,1,0:T(8,128)(2,1)} all-to-all(bf16[128,64,128]{2,1,0:T(8,128)(2,1)} %bitcast.48), channel_id=1, replica_groups=mesh['grp'=2,'wa'=128] {'wa'}, dimensions={0} | all-to-all | bytes 4194304 | tf_op jit(solution)/shard_map/all_to_all | solution.py:255
  117.1 12.4 %shard_map.104 = (bf16[128,1024]{1,0:T(8,128)(2,1)}, bf16[128,4096]{1,0:T(8,128)(2,1)}) custom-call(s32[64,128]{1,0:T(8,128)} %get-tuple-element.12.bag_ref, bf16[8192,128]{1,0:T(8,128)(2,1)} %bitcast.47, bf16[1024,4096]{1,0:T(8,128)(2,1)} %w_ref.3), custom_call_target="tpu_custom_call" | custom-call | flops 3221225472 | bytes 12582912 | tf_op jit(solution)/shard_map/pallas_call | solution.py:258
  129.5 2.5 collective-permute-start
  134.0 21.6 %collective-permute-done.other_ref = bf16[128,4096]{1,0:T(8,128)(2,1)S(1)} collective-permute-done((bf16[128,4096]{1,0:T(8,128)(2,1)}, bf16[128,4096]{1,0:T(8,128)(2,1)S(1)}, u32[]{:S(2)}, u32[]{:S(2)}) %collective-permute-start) | collective-permute-done | bytes 1048608 | tf_op jit(solution)/shard_map/ppermute | solution.py:264
  156.5 4.1 %shard_map.105 = (f32[128,1]{1,0:T(8,128)}, bf16[8,128,512]{2,1,0:T(8,128)(2,1)}, f32[1,4096]{1,0:T(1,128)}) custom-call(bf16[128,4096]{1,0:T(8,128)(2,1)} %get-tuple-element.14.mine_ref, bf16[128,4096]{1,0:T(8,128)(2,1)} %copy-done.2, f32[128,1]{1,0:T(8,128)} %copy.17.labels_ref, bf16[1,4096]{1,0:T(2,128)(2,1)} %reshape.66.w_head_ref), custom_call_target="tpu_custom_call" | custom-call | flops 31457280 | bytes 4194304 | tf_op jit(solution)/shard_map/pallas_call | solution.py:270
  163.6 2.5 collective-permute-start.3
  170.2 7.9 %collective-permute-done.2.refs_1_ = bf16[256,1024]{1,0:T(8,128)(2,1)S(1)} collective-permute-done((bf16[256,1024]{1,0:T(8,128)(2,1)S(1)}, bf16[256,1024]{1,0:T(8,128)(2,1)S(1)}, u32[]{:S(2)}, u32[]{:S(2)}) %collective-permute-start.2) | collective-permute-done | bytes 524320 | tf_op jit(solution)/shard_map/ppermute | solution.py:268
  178.8 8.8 %collective-permute-done.3.refs_2_ = bf16[256,1024]{1,0:T(8,128)(2,1)S(1)} collective-permute-done((bf16[256,1024]{1,0:T(8,128)(2,1)S(1)}, bf16[256,1024]{1,0:T(8,128)(2,1)S(1)}, u32[]{:S(2)}, u32[]{:S(2)}) %collective-permute-start.3) | collective-permute-done | bytes 524320 | tf_op jit(solution)/shard_map/ppermute | solution.py:268
  189.8 5.2 %collective-permute-done.6.refs_5_ = bf16[256,512]{1,0:T(8,128)(2,1)S(1)} collective-permute-done((bf16[256,512]{1,0:T(8,128)(2,1)}, bf16[256,512]{1,0:T(8,128)(2,1)S(1)}, u32[]{:S(2)}, u32[]{:S(2)}) %collective-permute-start.6) | collective-permute-done | bytes 262176 | tf_op jit(solution)/shard_map/ppermute | solution.py:290
  195.0 4.4 %collective-permute-done.7.refs_6_ = bf16[256,512]{1,0:T(8,128)(2,1)S(1)} collective-permute-done((bf16[256,512]{1,0:T(8,128)(2,1)S(1)}, bf16[256,512]{1,0:T(8,128)(2,1)S(1)}, u32[]{:S(2)}, u32[]{:S(2)}) %collective-permute-start.7) | collective-permute-done | bytes 262176 | tf_op jit(solution)/shard_map/ppermute | solution.py:290
  201.6 4.1 %shard_map.106 = bf16[1024,512]{1,0:T(8,128)(2,1)} custom-call(bf16[256,1024]{1,0:T(8,128)(2,1)} %copy-done.1, bf16[256,1024]{1,0:T(8,128)(2,1)} %copy-done.3, bf16[256,1024]{1,0:T(8,128)(2,1)} %copy-done.4, bf16[256,1024]{1,0:T(8,128)(2,1)} %collective-permute-done.4.refs_3_, bf16[256,512]{1,0:T(8,128)(2,1)} %get-tuple-element.21.refs_4_, ...), custom_call_target="tpu_custom_call" | custom-call | flops 1073741824 | bytes 4194304 | tf_op jit(solution)/shard_map/pallas_call | solution.py:303
  208.7 11.5 %collective-permute-done.9 = bf16[8,64,512]{2,1,0:T(8,128)(2,1)S(1)} collective-permute-done((bf16[8,64,512]{2,1,0:T(8,128)(2,1)S(1)}, bf16[8,64,512]{2,1,0:T(8,128)(2,1)S(1)}, u32[]{:S(2)}, u32[]{:S(2)}) %collective-permute-start.9) | collective-permute-done | bytes 524320 | tf_op jit(solution)/shard_map/ppermute | solution.py:308
  222.1 3.5 all-to-all-start.2
  226.4 15.1 %all-to-all-done.2 = bf16[8,64,512]{2,1,0:T(8,128)(2,1)S(1)} async-done(((bf16[8,64,512]{2,1,0:T(8,128)(2,1)}), bf16[8,64,512]{2,1,0:T(8,128)(2,1)S(1)}, u32[]{:S(2)}, u32[]{:S(2)}) %all-to-all-start.2) | async-done | bytes 524320 | tf_op jit(solution)/shard_map/all_to_all | solution.py:310
  241.5 8.2 %all-to-all-start.4 = ((f32[128,1,16]{2,1,0:T(1,128)}), f32[128,1,16]{2,1,0:T(1,128)S(1)}, u32[]{:S(2)}, u32[]{:S(2)}) async-start(f32[128,1,16]{2,1,0:T(1,128)} %bitcast.23), calls=%async_computation.4 | async-start | bytes 131072 | tf_op jit(solution)/shard_map/all_to_all | solution.py:316
  250.4 9.8 %all-to-all-done.4 = f32[128,1,16]{2,1,0:T(1,128)S(1)} async-done(((f32[128,1,16]{2,1,0:T(1,128)}), f32[128,1,16]{2,1,0:T(1,128)S(1)}, u32[]{:S(2)}, u32[]{:S(2)}) %all-to-all-start.4) | async-done | bytes 8224 | tf_op jit(solution)/shard_map/all_to_all | solution.py:316
  260.2 3.9 %all-to-all-start.3 = ((f32[8,8,512]{2,1,0:T(8,128)}), f32[8,8,512]{2,1,0:T(8,128)S(1)}, u32[]{:S(2)}, u32[]{:S(2)}) async-start(f32[8,8,512]{2,1,0:T(8,128)} %bitcast.20), calls=%async_computation.3 | async-start | bytes 262144 | tf_op jit(solution)/shard_map/all_to_all | solution.py:312
  264.1 12.1 %shard_map.107 = bf16[8192,128]{1,0:T(8,128)(2,1)} custom-call(bf16[8,128,512]{2,1,0:T(8,128)(2,1)} %get-tuple-element.17.grad_ref, bf16[1024,4096]{1,0:T(8,128)(2,1)} %w_ref.3, s32[128,64]{1,0:T(8,128)} %get-tuple-element.19.bag_t_ref), custom_call_target="tpu_custom_call" | custom-call | flops 3221225472 | bytes 12582912 | tf_op jit(solution)/shard_map/pallas_call | solution.py:292
  276.3 6.6 %all-to-all-start.5 = ((bf16[128,64,128]{2,1,0:T(8,128)(2,1)}), bf16[128,64,128]{2,1,0:T(8,128)(2,1)S(1)}, u32[]{:S(2)}, u32[]{:S(2)}) async-start(bf16[128,64,128]{2,1,0:T(8,128)(2,1)} %bitcast.45), calls=%async_computation.5 | async-start | bytes 4194304 | tf_op jit(solution)/shard_map/all_to_all | solution.py:299
  286.2 48.0 %all-to-all-done.5 = bf16[128,64,128]{2,1,0:T(8,128)(2,1)S(1)} async-done(((bf16[128,64,128]{2,1,0:T(8,128)(2,1)}), bf16[128,64,128]{2,1,0:T(8,128)(2,1)S(1)}, u32[]{:S(2)}, u32[]{:S(2)}) %all-to-all-start.5) | async-done | bytes 2097184 | tf_op jit(solution)/shard_map/all_to_all | solution.py:299
  335.5 27.1 %shard_map.108 = bf16[4096,128]{1,0:T(8,128)(2,1)} custom-call(s32[64,128]{1,0:T(8,128)} %reshape.72.ids_ref, bf16[8192,128]{1,0:T(8,128)(2,1)} %bitcast.46), custom_call_target="tpu_custom_call" | custom-call | flops 8589934592 | bytes 4194304 | tf_op jit(solution)/shard_map/pallas_call | solution.py:321
  (60 shorter events, 28.1 us)
Async XLA Ops:
  117.1 15.5 %copy-start.13 = (f32[128]{0:T(128)S(1)}, f32[128]{0:T(128)}, u32[]{:S(2)}) copy-start(f32[128]{0:T(128)} %param.11) | copy-start | bytes 1540
  117.1 16.3 %copy-start.11 = (bf16[4096]{0:T(1024)(128)(2,1)S(1)}, bf16[4096]{0:T(1024)(128)(2,1)}, u32[]{:S(2)}) copy-start(bf16[4096]{0:T(1024)(128)(2,1)} %param.13) | copy-start | bytes 24580
  129.5 26.1 %collective-permute-start = (bf16[128,4096]{1,0:T(8,128)(2,1)}, bf16[128,4096]{1,0:T(8,128)(2,1)S(1)}, u32[]{:S(2)}, u32[]{:S(2)}) collective-permute-start(bf16[128,4096]{1,0:T(8,128)(2,1)} %get-tuple-element.14.mine_ref), channel_id=1, source_target_pairs={{0,128},{128,0},{1,129},{129,1},{2,130},{130,2},{3,131},{131,3},{4... | collective-permute-start | bytes 3145736 | tf_op jit(solution)/shard_map/ppermute | solution.py:264
  131.9 31.4 %collective-permute-start.1 = (bf16[128,1024]{1,0:T(8,128)(2,1)}, bf16[128,1024]{1,0:T(8,128)(2,1)S(1)}, u32[]{:S(2)}, u32[]{:S(2)}) collective-permute-start(bf16[128,1024]{1,0:T(8,128)(2,1)} %get-tuple-element.16), channel_id=1, source_target_pairs={{0,1},{1,0},{2,3},{3,2},{4,5},{5,4},{6,7},{7,6},{8,9},{9,8},{10,11... | collective-permute-start | bytes 786440 | tf_op jit(solution)/shard_map/ppermute | solution.py:266
  134.0 29.3 %copy-start.8 = (bf16[128,1024]{1,0:T(8,128)(2,1)S(1)}, bf16[128,1024]{1,0:T(8,128)(2,1)}, u32[]{:S(2)}) copy-start(bf16[128,1024]{1,0:T(8,128)(2,1)} %get-tuple-element.16) | copy-start | bytes 786436
  162.0 4.7 %collective-permute-start.5 = (bf16[4,128,512]{2,1,0:T(8,128)(2,1)S(1)}, bf16[4,128,512]{2,1,0:T(8,128)(2,1)S(1)}, u32[]{:S(2)}, u32[]{:S(2)}) collective-permute-start(bf16[4,128,512]{2,1,0:T(8,128)(2,1)S(1)} %get-tuple-element.24), channel_id=1, source_target_pairs={{0,1},{1,0},{2,3},{3,2},{4,5},{5,4},{6,7},{7,6},{8,9},{9,8},{10,11... | collective-permute-start | bytes 1572872 | tf_op jit(solution)/shard_map/ppermute | solution.py:284
  163.3 37.6 %copy-start.1 = (bf16[256,1024]{1,0:T(8,128)(2,1)}, bf16[256,1024]{1,0:T(8,128)(2,1)S(1)}, u32[]{:S(2)}) copy-start(bf16[256,1024]{1,0:T(8,128)(2,1)S(1)} %constant_dynamic-update-slice_fusion.refs_0_) | copy-start | bytes 1572868
  163.4 14.8 %collective-permute-start.2 = (bf16[256,1024]{1,0:T(8,128)(2,1)S(1)}, bf16[256,1024]{1,0:T(8,128)(2,1)S(1)}, u32[]{:S(2)}, u32[]{:S(2)}) collective-permute-start(bf16[256,1024]{1,0:T(8,128)(2,1)S(1)} %constant_dynamic-update-slice_fusion.refs_0_), channel_id=1, source_target_pairs={{0,2},{1,3},{2,4},{3,5},{4,6},{5,7},{6,0},{7,1},{8,10},{9,11},{10,... | collective-permute-start | bytes 1572872 | tf_op jit(solution)/shard_map/ppermute | solution.py:268
  163.6 24.1 %collective-permute-start.3 = (bf16[256,1024]{1,0:T(8,128)(2,1)S(1)}, bf16[256,1024]{1,0:T(8,128)(2,1)S(1)}, u32[]{:S(2)}, u32[]{:S(2)}) collective-permute-start(bf16[256,1024]{1,0:T(8,128)(2,1)S(1)} %constant_dynamic-update-slice_fusion.refs_0_), channel_id=1, source_target_pairs={{0,6},{1,7},{2,0},{3,1},{4,2},{5,3},{6,4},{7,5},{8,14},{9,15},{10,... | collective-permute-start | bytes 1572872 | tf_op jit(solution)/shard_map/ppermute | solution.py:268
  166.1 23.7 %collective-permute-start.4 = (bf16[256,1024]{1,0:T(8,128)(2,1)S(1)}, bf16[256,1024]{1,0:T(8,128)(2,1)}, u32[]{:S(2)}, u32[]{:S(2)}) collective-permute-start(bf16[256,1024]{1,0:T(8,128)(2,1)S(1)} %constant_dynamic-update-slice_fusion.refs_0_), channel_id=1, source_target_pairs={{0,4},{1,5},{2,6},{3,7},{4,0},{5,1},{6,2},{7,3},{8,12},{9,13},{10,... | collective-permute-start | bytes 1572872 | tf_op jit(solution)/shard_map/ppermute | solution.py:268
  167.6 27.5 %collective-permute-start.6 = (bf16[256,512]{1,0:T(8,128)(2,1)}, bf16[256,512]{1,0:T(8,128)(2,1)S(1)}, u32[]{:S(2)}, u32[]{:S(2)}) collective-permute-start(bf16[256,512]{1,0:T(8,128)(2,1)} %get-tuple-element.22), channel_id=1, source_target_pairs={{0,2},{1,3},{2,4},{3,5},{4,6},{5,7},{6,0},{7,1},{8,10},{9,11},{10,... | collective-permute-start | bytes 786440 | tf_op jit(solution)/shard_map/ppermute | solution.py:290
  168.1 31.4 %collective-permute-start.7 = (bf16[256,512]{1,0:T(8,128)(2,1)S(1)}, bf16[256,512]{1,0:T(8,128)(2,1)S(1)}, u32[]{:S(2)}, u32[]{:S(2)}) collective-permute-start(bf16[256,512]{1,0:T(8,128)(2,1)S(1)} %get-tuple-element.23), channel_id=1, source_target_pairs={{0,6},{1,7},{2,0},{3,1},{4,2},{5,3},{6,4},{7,5},{8,14},{9,15},{10,... | collective-permute-start | bytes 786440 | tf_op jit(solution)/shard_map/ppermute | solution.py:290
  178.2 22.7 %copy-start.3 = (bf16[256,1024]{1,0:T(8,128)(2,1)}, bf16[256,1024]{1,0:T(8,128)(2,1)S(1)}, u32[]{:S(2)}) copy-start(bf16[256,1024]{1,0:T(8,128)(2,1)S(1)} %collective-permute-done.2.refs_1_) | copy-start | bytes 1572868
  178.2 22.7 %collective-permute-start.8 = (bf16[256,512]{1,0:T(8,128)(2,1)S(1)}, bf16[256,512]{1,0:T(8,128)(2,1)S(1)}, u32[]{:S(2)}, u32[]{:S(2)}) collective-permute-start(bf16[256,512]{1,0:T(8,128)(2,1)S(1)} %get-tuple-element.20), channel_id=1, source_target_pairs={{0,4},{1,5},{2,6},{3,7},{4,0},{5,1},{6,2},{7,3},{8,12},{9,13},{10,... | collective-permute-start | bytes 786440 | tf_op jit(solution)/shard_map/ppermute | solution.py:290
  187.7 13.3 %copy-start.4 = (bf16[256,1024]{1,0:T(8,128)(2,1)}, bf16[256,1024]{1,0:T(8,128)(2,1)S(1)}, u32[]{:S(2)}) copy-start(bf16[256,1024]{1,0:T(8,128)(2,1)S(1)} %collective-permute-done.3.refs_2_) | copy-start | bytes 1572868
  195.0 5.9 %copy-start.5 = (bf16[256,512]{1,0:T(8,128)(2,1)}, bf16[256,512]{1,0:T(8,128)(2,1)S(1)}, u32[]{:S(2)}) copy-start(bf16[256,512]{1,0:T(8,128)(2,1)S(1)} %collective-permute-done.6.refs_5_) | copy-start | bytes 786436
  205.7 20.0 %copy-start.12 = (f32[1,4096]{1,0:T(1,128)S(1)}, f32[1,4096]{1,0:T(1,128)}, u32[]{:S(2)}) copy-start(f32[1,4096]{1,0:T(1,128)} %get-tuple-element.18) | copy-start | bytes 49156
  206.8 13.4 %collective-permute-start.9 = (bf16[8,64,512]{2,1,0:T(8,128)(2,1)S(1)}, bf16[8,64,512]{2,1,0:T(8,128)(2,1)S(1)}, u32[]{:S(2)}, u32[]{:S(2)}) collective-permute-start(bf16[8,64,512]{2,1,0:T(8,128)(2,1)S(1)} %dynamic-slice_bitcast_fusion), channel_id=1, source_target_pairs={{0,8},{1,9},{2,10},{3,11},{4,12},{5,13},{6,14},{7,15},{8,0},{9,1},... | collective-permute-start | bytes 1572872 | tf_op jit(solution)/shard_map/ppermute | solution.py:308
  222.1 19.3 %all-to-all-start.2 = ((bf16[8,64,512]{2,1,0:T(8,128)(2,1)}), bf16[8,64,512]{2,1,0:T(8,128)(2,1)S(1)}, u32[]{:S(2)}, u32[]{:S(2)}) async-start(bf16[8,64,512]{2,1,0:T(8,128)(2,1)} %fusion), calls=%async_computation.2 | async-start | bytes 1048576 | tf_op jit(solution)/shard_map/all_to_all | solution.py:310
  241.5 18.7 %all-to-all-start.4 = ((f32[128,1,16]{2,1,0:T(1,128)}), f32[128,1,16]{2,1,0:T(1,128)S(1)}, u32[]{:S(2)}, u32[]{:S(2)}) async-start(f32[128,1,16]{2,1,0:T(1,128)} %bitcast.23), calls=%async_computation.4 | async-start | bytes 131072 | tf_op jit(solution)/shard_map/all_to_all | solution.py:316
  260.2 16.1 %all-to-all-start.3 = ((f32[8,8,512]{2,1,0:T(8,128)}), f32[8,8,512]{2,1,0:T(8,128)S(1)}, u32[]{:S(2)}, u32[]{:S(2)}) async-start(f32[8,8,512]{2,1,0:T(8,128)} %bitcast.20), calls=%async_computation.3 | async-start | bytes 262144 | tf_op jit(solution)/shard_map/all_to_all | solution.py:312
  276.3 7.1 %copy-start.9 = (s32[128,1,64]{2,1,0:T(1,128)S(1)}, s32[128,1,64]{2,1,0:T(1,128)}, u32[]{:S(2)}) copy-start(s32[128,1,64]{2,1,0:T(1,128)} %all_to_all.40) | copy-start | bytes 98308
  276.3 8.6 %copy-start.10 = (f32[128,1]{1,0:T(8,128)S(1)}, f32[128,1]{1,0:T(8,128)}, u32[]{:S(2)}) copy-start(f32[128,1]{1,0:T(8,128)} %get-tuple-element.15) | copy-start | bytes 1540
  276.3 57.9 %all-to-all-start.5 = ((bf16[128,64,128]{2,1,0:T(8,128)(2,1)}), bf16[128,64,128]{2,1,0:T(8,128)(2,1)S(1)}, u32[]{:S(2)}, u32[]{:S(2)}) async-start(bf16[128,64,128]{2,1,0:T(8,128)(2,1)} %bitcast.45), calls=%async_computation.5 | async-start | bytes 4194304 | tf_op jit(solution)/shard_map/all_to_all | solution.py:299
  (4 other events, 4.5 us)
